TPU v7x, 512 devices: a whole 4x8x8 slice. The times are simulated.
512 devices in a mesh: kv: 8 (over y), seq: 64 (over z, x, core).
Axes of the slice: x: 4, y: 8, z: 8, core: 2. Of those that a mesh axis runs over, the one named last changes fastest.
Arguments:
- queries: bfloat16 [128, 8192], P('seq', 'kv'), may hold values from -8 to 8
- owner_slot: int32 [128], replicated, may hold values from 0 to 127, each once
- suffix_len: int32 [128], P('seq'), may hold values from 1 to 256, as said below
- prompt_keys: bfloat16 [32768, 1024], P('seq', 'kv'), may hold values from -8 to 8
- prompt_value_rows: bfloat16 [32768, 1024], P('seq', 'kv'), may hold values from -6 to 6
- key_scale: float32 [256, 8], P('seq', 'kv'), may hold values from 0.5 to 3
- value_block_scale: float32 [256, 8], P('seq', 'kv'), may hold values from 0.5 to 2
- suffix_key_rows: bfloat16 [128, 256, 1024], P('seq', None, 'kv'), may hold values from -16 to 16
- suffix_value_rows: bfloat16 [128, 256, 1024], P('seq', None, 'kv'), may hold values from -6 to 6
- out_weight: bfloat16 [8192, 5120], P('kv', 'seq'), may hold values from -0.0625 to 0.0625
Outputs:
- layer_out: float32 [128, 5120], P('kv', 'seq')
Inputs may be any that keep to these rules, and one draw needn't show every extreme that they name: `owner_slot`: each slot appears once; slot i belongs to index i // 2 of seq. Slot i's suffix occupies positions 0 to suffix_len[i] - 1; some slot has all 256.
All inputs are finite; a program needn't handle non-finite values.
Results may differ from a plain program's by a relative error of at most 0.0055.
Values may be sent and summed in bfloat16 or wider, within the bound.
A program may use at most 192 MiB of HBM per device.

v0:
```python
import jax
import jax.numpy as jnp
from jax import lax
from jax.sharding import PartitionSpec as P

HEAD_WIDTH = 128
GROUP = 8
SCALE_SPAN = 128


NEG_FILL = -1e30


def combine_parts(earlier, later):
    numer_a, peak_a, weight_a = earlier
    numer_b, peak_b, weight_b = later
    peak = jnp.maximum(peak_a, peak_b)
    factor_a = jnp.exp(peak_a - peak)
    factor_b = jnp.exp(peak_b - peak)
    return (
        numer_a * factor_a[..., None] + numer_b * factor_b[..., None],
        peak,
        weight_a * factor_a + weight_b * factor_b,
    )


def fold_sources(received):
    numerator, peak, weight_sum = received
    row_peak = jnp.max(peak, axis=0)
    factor = jnp.exp(peak - row_peak[None])
    return (
        jnp.sum(numerator * factor[..., None], axis=0),
        row_peak,
        jnp.sum(weight_sum * factor, axis=0),
    )


def prompt_block(block_queries, key_rows, value_rows, key_factor, value_factor):
    row_count = block_queries.shape[0] * GROUP
    flat_queries = block_queries.reshape(row_count, HEAD_WIDTH)
    blocks = key_rows.shape[0] // SCALE_SPAN
    scores = jnp.einsum("rd,td->rt", flat_queries, key_rows, preferred_element_type=jnp.float32)
    scores = (scores.reshape(row_count, blocks, SCALE_SPAN) * key_factor[None, :, None]).reshape(
        row_count, blocks * SCALE_SPAN
    )
    peak = jnp.max(scores, axis=1)
    weights = jnp.exp(scores - peak[:, None])
    weight_sum = jnp.sum(weights, axis=1)
    scaled = (
        (weights.reshape(row_count, blocks, SCALE_SPAN) * value_factor[None, :, None])
        .reshape(row_count, blocks * SCALE_SPAN)
        .astype(jnp.bfloat16)
    )
    numerator = jnp.dot(scaled, value_rows, preferred_element_type=jnp.float32)
    return (
        numerator.reshape(-1, GROUP, HEAD_WIDTH),
        peak.reshape(-1, GROUP),
        weight_sum.reshape(-1, GROUP),
    )


def suffix_part(own_queries, suffix_key_rows, suffix_value_rows, suffix_len):
    samples = own_queries.shape[0]
    head_queries = own_queries.reshape(samples, GROUP, HEAD_WIDTH)
    scores = jnp.einsum(
        "sjd,sud->sju", head_queries, suffix_key_rows, preferred_element_type=jnp.float32
    ) * HEAD_WIDTH ** (-0.5)
    live_mask = (
        jnp.arange(suffix_key_rows.shape[1], dtype=jnp.int32)[None, None, :]
        < suffix_len[:, None, None]
    )
    scores = jnp.where(live_mask, scores, NEG_FILL)
    peak = jnp.max(scores, axis=2)
    weights = jnp.where(live_mask, jnp.exp(scores - peak[..., None]), 0.0)
    weight_sum = jnp.sum(weights, axis=2)
    numerator = jnp.einsum(
        "sju,sud->sjd",
        weights.astype(jnp.bfloat16),
        suffix_value_rows,
        preferred_element_type=jnp.float32,
    )
    return (numerator, peak, weight_sum)


def local(
    queries,
    owner_slot,
    suffix_len,
    prompt_keys,
    prompt_value_rows,
    key_scale,
    value_block_scale,
    suffix_key_rows,
    suffix_value_rows,
    out_weight,
):
    owners = lax.axis_size("seq")
    own_index = lax.axis_index("seq")
    own_count = queries.shape[0]
    total_count = own_count * owners
    gathered = lax.all_gather(queries, "seq", axis=0, tiled=True)
    slot_sample = (
        jnp.zeros((total_count,), jnp.int32)
        .at[owner_slot]
        .set(jnp.arange(total_count, dtype=jnp.int32))
    )
    slot_queries = gathered[slot_sample]
    sample_span = min(total_count, max(1, 512 // GROUP))
    key_factor = key_scale[:, 0] * HEAD_WIDTH ** (-0.5)
    value_factor = value_block_scale[:, 0]

    def one_block(block_queries):
        return prompt_block(block_queries, prompt_keys, prompt_value_rows, key_factor, value_factor)

    numerator, peak, weight_sum = lax.map(
        one_block, slot_queries.reshape(total_count // sample_span, sample_span, GROUP * HEAD_WIDTH)
    )
    numerator = numerator.reshape(total_count, GROUP, HEAD_WIDTH)
    peak = peak.reshape(total_count, GROUP)
    weight_sum = weight_sum.reshape(total_count, GROUP)
    own_first = own_index * own_count
    own_queries = lax.dynamic_slice_in_dim(slot_queries, own_first, own_count, 0)
    recent = suffix_part(own_queries, suffix_key_rows, suffix_value_rows, suffix_len)
    outgoing_numer = numerator.reshape(owners, own_count, GROUP, HEAD_WIDTH)
    outgoing_peak = peak.reshape(owners, own_count, GROUP)
    outgoing_weight = weight_sum.reshape(owners, own_count, GROUP)
    arrived = fold_sources(
        (
            lax.all_to_all(outgoing_numer, "seq", split_axis=0, concat_axis=0, tiled=True),
            lax.all_to_all(outgoing_peak, "seq", split_axis=0, concat_axis=0, tiled=True),
            lax.all_to_all(outgoing_weight, "seq", split_axis=0, concat_axis=0, tiled=True),
        )
    )
    numer_own, peak_own, weight_own = combine_parts(arrived, recent)
    attention_own = (
        (numer_own / weight_own[..., None])
        .reshape(own_count, GROUP * HEAD_WIDTH)
        .astype(jnp.bfloat16)
    )
    partial_value = jnp.dot(
        lax.all_gather(attention_own, "seq", axis=0, tiled=True),
        out_weight,
        preferred_element_type=jnp.float32,
    )
    return lax.psum_scatter(partial_value, "kv", scatter_dimension=0, tiled=True)


def solution(mesh):
    in_specs = (
        P("seq", "kv"),
        P(),
        P("seq"),
        P("seq", "kv"),
        P("seq", "kv"),
        P("seq", "kv"),
        P("seq", "kv"),
        P("seq", None, "kv"),
        P("seq", None, "kv"),
        P("kv", "seq"),
    )
    out_specs = P("kv", "seq")
    return jax.shard_map(local, mesh=mesh, in_specs=in_specs, out_specs=out_specs, check_vma=False)
```

profile of v0, /device:TPU:2, one launch (start us, length us, event | category | flops | bytes accessed | tf_op | source)
XLA Modules:
  0.0 208.1 jit_solution(6570594273177355561)
XLA Ops:
  6.5 0.7 copy-done.5
  7.3 49.9 %all-gather = bf16[64,2,1024]{2,1,0:T(2,128)(2,1)S(1)} all-gather(bf16[1,2,1024]{2,1,0:T(2,128)(2,1)S(1)} %bitcast.49), channel_id=1, replica_groups=mesh['kv'=8,'seq'=64] {'seq'}, dimensions={0}, use_global_device_ids=true | all-gather | bytes 266240 | tf_op jit(solution)/shard_map/all_gather | solution.py:101
  57.3 0.6 copy-done.7
  57.9 1.0 scatter_custom_fusion
  58.9 0.6 copy-done.8
  59.5 0.9 gather_fusion
  60.5 0.6 copy-done.4
  61.1 6.0 %while.14 = (s32[]{:T(128)}, f32[2,64,8,128]{3,2,1,0:T(8,128)}, f32[2,64,8]{2,1,0:T(8,128)}, f32[2,64,8]{2,1,0:T(8,128)S(1)}, bf16[2,64,1024]{2,1,0:T(8,128)(2,1...) while((s32[]{:T(128)}, f32[2,64,8,128]{3,2,1,0:T(8,128)}, ...), condition=%wide.region_4.5_spmd, body=%wide.region_1.4_spmd.sunk | while | flops 135789568 | bytes 6568089 | solution.py:115
  61.1 0.3 fusion.43
  61.5 0.3 fusion.44
  61.7 0.3 copy.22
  62.0 0.2 convert_element_type.27
  62.2 1.0 fusion.45
  63.4 0.6 constant_dynamic-update-slice_fusion.3
  64.1 0.3 fusion.43
  64.4 0.3 fusion.44
  64.7 0.3 copy.22
  65.0 0.2 convert_element_type.27
  65.2 1.0 fusion.45
  66.4 0.6 constant_dynamic-update-slice_fusion.3
  67.0 14.7 %all_to_all.15 = f32[64,2,8]{2,1,0:T(2,128)S(1)} all-to-all(f32[64,2,8]{2,1,0:T(2,128)S(1)} %bitcast.47), channel_id=1, replica_groups=mesh['kv'=8,'seq'=64] {'seq'}, dimensions={0} | all-to-all | bytes 8192 | tf_op jit(solution)/shard_map/all_to_all | solution.py:131
  81.7 5.6 %all-to-all-start.1 = ((f32[64,2,8]{2,1,0:T(2,128)}), f32[64,2,8]{2,1,0:T(2,128)S(1)}, u32[]{:S(2)}, u32[]{:S(2)}) async-start(f32[64,2,8]{2,1,0:T(2,128)} %bitcast.8), calls=%async_computation.1 | async-start | bytes 131072 | tf_op jit(solution)/shard_map/all_to_all | solution.py:130
  87.4 9.0 %all-to-all-done.1 = f32[64,2,8]{2,1,0:T(2,128)S(1)} async-done(((f32[64,2,8]{2,1,0:T(2,128)}), f32[64,2,8]{2,1,0:T(2,128)S(1)}, u32[]{:S(2)}, u32[]{:S(2)}) %all-to-all-start.1) | async-done | bytes 4128 | tf_op jit(solution)/shard_map/all_to_all | solution.py:130
  96.4 5.7 %all-to-all-start = ((f32[64,2,8,128]{3,2,1,0:T(8,128)}), f32[64,2,8,128]{3,2,1,0:T(8,128)S(1)}, u32[]{:S(2)}, u32[]{:S(2)}) async-start(f32[64,2,8,128]{3,2,1,0:T(8,128)} %bitcast.7), calls=%async_computation | async-start | bytes 1048576 | tf_op jit(solution)/shard_map/all_to_all | solution.py:129
  102.2 0.6 copy-done.9
  102.9 0.2 fusion.23
  103.4 16.4 %all-to-all-done = f32[64,2,8,128]{3,2,1,0:T(8,128)S(1)} async-done(((f32[64,2,8,128]{3,2,1,0:T(8,128)}), f32[64,2,8,128]{3,2,1,0:T(8,128)S(1)}, u32[]{:S(2)}, u32[]{:S(2)}) %all-to-all-start) | async-done | bytes 524320 | tf_op jit(solution)/shard_map/all_to_all | solution.py:129
  119.8 0.2 multiply_reduce_fusion
  120.0 0.7 copy-done.6
  120.9 41.8 %all-gather.1 = bf16[64,2,1024]{2,1,0:T(2,128)(2,1)S(1)} all-gather(bf16[1,2,1024]{2,1,0:T(2,128)(2,1)S(1)} %reshape.116), channel_id=1, replica_groups=mesh['kv'=8,'seq'=64] {'seq'}, dimensions={0}, use_global_device_ids=true | all-gather | bytes 266240 | tf_op jit(solution)/shard_map/all_gather | solution.py:141
  162.8 0.8 fusion.24
  163.6 37.6 %reduce-scatter.2.cloned.1.call-done = f32[16,80]{1,0:T(8,128)} async-done(((f32[128,80]{1,0:T(8,128)}), f32[16,80]{1,0:T(8,128)}) %reduce-scatter.2.cloned.1.call-update) | async-done | bytes 5136 | tf_op jit(solution)/shard_map/reduce_scatter | solution.py:145
  (42 shorter events, 1.5 us)
Async XLA Ops:
  6.5 156.2 %copy-start = (bf16[1024,80]{0,1:T(8,128)(2,1)S(1)}, bf16[1024,80]{0,1:T(8,128)(2,1)}, u32[]{:S(2)}) copy-start(bf16[1024,80]{0,1:T(8,128)(2,1)} %param.21) | copy-start | bytes 491524
  6.5 0.7 copy-start.5
  57.2 0.7 copy-start.7
  58.9 0.7 copy-start.8
  59.5 0.9 copy-start.1
  59.5 1.0 copy-start.2
  60.4 0.7 copy-start.4
  81.7 14.6 %all-to-all-start.1 = ((f32[64,2,8]{2,1,0:T(2,128)}), f32[64,2,8]{2,1,0:T(2,128)S(1)}, u32[]{:S(2)}, u32[]{:S(2)}) async-start(f32[64,2,8]{2,1,0:T(2,128)} %bitcast.8), calls=%async_computation.1 | async-start | bytes 131072 | tf_op jit(solution)/shard_map/all_to_all | solution.py:130
  96.4 6.5 %copy-start.3 = (bf16[2,256,128]{2,1,0:T(8,128)(2,1)S(1)}, bf16[2,256,128]{2,1,0:T(8,128)(2,1)}, u32[]{:S(2)}) copy-start(bf16[2,256,128]{2,1,0:T(8,128)(2,1)} %param.19) | copy-start | bytes 393220
  96.4 23.4 %all-to-all-start = ((f32[64,2,8,128]{3,2,1,0:T(8,128)}), f32[64,2,8,128]{3,2,1,0:T(8,128)S(1)}, u32[]{:S(2)}, u32[]{:S(2)}) async-start(f32[64,2,8,128]{3,2,1,0:T(8,128)} %bitcast.7), calls=%async_computation | async-start | bytes 1048576 | tf_op jit(solution)/shard_map/all_to_all | solution.py:129
  102.1 0.7 copy-start.9
  102.1 99.1 %reduce-scatter.2.cloned.1.call-start = ((), (), s32[]{:S(2)}) async-start(), calls=%async_computation.4 | async-start | bytes 73728 | tf_op jit(solution)/shard_map/reduce_scatter | solution.py:145
  119.8 0.9 copy-start.6
Sparse Core Ops, SparseCore 0:
  163.8 37.4 reduce-scatter.1
where the time goes:
time: 208 us
  blocking collectives  106 us (51%)
  waiting for transfers between devices  63 us (30%)
  between operations  13.5 us (6%)
  starting transfers between devices  11.4 us (5%)
  local copies, waits for them, and re-layouts  8.66 us (4%)
  matrix products  3.89 us (2%)
    all_gather x1, blocking collectives, local(): gathered = lax.all_gather(queries, 'seq', axis=0, tiled=True)  49.9 us
    all_gather x1, blocking collectives, local(): lax.all_gather(attention_own, 'seq', axis=0, tiled=True)  41.8 us
    reduce_scatter x1, waiting for transfers between devices, local(): lax.psum_scatter(partial_value, 'kv', scatter_dimension=0, tiled=True)  37.6 us
    all_to_all x1, waiting for transfers between devices, local(): lax.all_to_all(outgoing_numer, 'seq', split_axis=0, concat_axis=0, tiled=...  16.4 us
    all_to_all x1, blocking collectives, local(): lax.all_to_all(outgoing_weight, 'seq', split_axis=0, concat_axis=0, tiled...  14.7 us
    all_to_all x1, waiting for transfers between devices, local(): lax.all_to_all(outgoing_peak, 'seq', split_axis=0, concat_axis=0, tiled=T...  9.02 us
    all_to_all x1, starting transfers between devices, local(): lax.all_to_all(outgoing_numer, 'seq', split_axis=0, concat_axis=0, tiled=...  5.73 us
    all_to_all x1, starting transfers between devices, local(): lax.all_to_all(outgoing_peak, 'seq', split_axis=0, concat_axis=0, tiled=T...  5.61 us
  transfers between devices with their start and end apart: 3, of which 3 were waited for; matrix products, arithmetic and copies ran while one was open for 0% of the time, Pallas kernels for 0%

commit v1 on v0

v1 whole, which is shorter than its diff:
```python
import functools

import jax
import jax.numpy as jnp
from jax import lax
from jax.experimental import pallas as pl
from jax.experimental.pallas import tpu as pltpu
from jax.sharding import PartitionSpec as P

MESH = pl.DeviceIdType.MESH
F32 = jnp.float32
BF16 = jnp.bfloat16
LOG2E = 1.4426950408889634
NEG_FILL = -1e30

CORES = 2
GROUP = 8
WIDTH = 128
OWN = 2
ROWS = OWN * GROUP
SPAN = 128

SQ, SC, SK, SV, SW, SF, SN, SS, SA, SY = range(10)
LQ, LO, LK, LV, LKS, LVS, LW, LSK, LSV, LSL = range(10)


def nt_dot(a, b):
    return lax.dot_general(a, b, (((1,), (1,)), ((), ())), preferred_element_type=F32)


def kernel(
    chips,
    groups,
    q_hbm,
    os_hbm,
    sl_hbm,
    k_hbm,
    v_hbm,
    ks_hbm,
    vs_hbm,
    sk_hbm,
    sv_hbm,
    w_hbm,
    o_ref,
    qown,
    osv,
    sls,
    kbuf,
    vbuf,
    ksv,
    vsv,
    scb,
    skb,
    svb,
    wbuf,
    q32,
    qg,
    qf32,
    qs32,
    nsend,
    ssend,
    nrecv,
    srecv,
    att,
    a32,
    ysend,
    yrecv,
    ssem,
    rsem,
    lsem,
):
    me = lax.axis_index("seq")
    y = lax.axis_index("kv")
    c = lax.rem(me, CORES)
    chip = me // CORES
    other = 1 - c

    def load(src, dst, i):
        cp = pltpu.make_async_copy(src, dst, lsem.at[i])
        cp.start()
        return cp

    def remote(src, dst, i, seq, kv):
        return pltpu.make_async_remote_copy(
            src_ref=src,
            dst_ref=dst,
            send_sem=ssem.at[i],
            recv_sem=rsem.at[i],
            device_id={"kv": kv, "seq": seq},
            device_id_type=MESH,
        )

    load_q = load(q_hbm, qown, LQ)
    load_o = load(os_hbm, osv, LO)
    load_ks = load(ks_hbm, ksv, LKS)
    load_vs = load(vs_hbm, vsv, LVS)
    load_k = load(k_hbm, kbuf.at[c], LK)
    load_v = load(v_hbm, vbuf.at[c], LV)
    load_w = load(w_hbm, wbuf.at[c], LW)
    load_sk = load(sk_hbm, skb, LSK)
    load_sv = load(sv_hbm, svb, LSV)
    load_sl = load(sl_hbm, sls, LSL)

    barrier = pltpu.get_barrier_semaphore()

    def greet(seq, kv):
        pl.semaphore_signal(barrier, inc=1, device_id={"kv": kv, "seq": seq}, device_id_type=MESH)

    def greet_plane(k, carry):
        greet(lax.rem(chip + k, chips) * CORES + c, y)
        return carry

    lax.fori_loop(1, chips, greet_plane, 0)

    def greet_column(k, carry):
        greet(chip * CORES + c, lax.rem(y + k, groups))
        greet(chip * CORES + other, lax.rem(y + k, groups))
        return carry

    lax.fori_loop(1, groups, greet_column, 0)
    greet(chip * CORES + other, y)

    load_q.wait()
    for h in range(GROUP):
        piece = qown[:, h * WIDTH : (h + 1) * WIDTH].astype(F32)
        for s in range(OWN):
            q32[s * GROUP + h : s * GROUP + h + 1, :] = piece[s : s + 1, :]
    qg[c, chip] = q32[...].astype(BF16)

    pl.semaphore_wait(barrier, (chips - 1) + 2 * (groups - 1) + 1)

    half = chips // 2

    def far_first(k):
        step = half - (k // 2)
        return lax.rem(jnp.where(lax.rem(k, 2) == 0, step, chips - step), chips)

    def send_queries(k, carry):
        t = lax.rem(chip + far_first(k), chips)
        remote(qg.at[c, chip], qg.at[c, chip], SQ, t * CORES + c, y).start()
        return carry

    lax.fori_loop(1, chips, send_queries, 0)

    partner = chip * CORES + other
    swap_k = remote(k_hbm, kbuf.at[c], SK, partner, y)
    swap_k.start()
    swap_v = remote(v_hbm, vbuf.at[c], SV, partner, y)
    swap_v.start()
    swap_w = remote(w_hbm, wbuf.at[c], SW, partner, y)
    swap_w.start()
    load_ks.wait()
    load_vs.wait()
    blocks = ksv.shape[0]
    scb[c, 0:blocks, :] = jnp.broadcast_to(ksv[...] * (WIDTH**-0.5 * LOG2E), (blocks, WIDTH))
    scb[c, blocks : 2 * blocks, :] = jnp.broadcast_to(vsv[...], (blocks, WIDTH))
    swap_f = remote(scb.at[c], scb.at[c], SF, partner, y)
    swap_f.start()

    load_o.wait()
    samples = chips * CORES * OWN
    slots = chips * OWN
    s_i = lax.broadcasted_iota(jnp.int32, (samples, samples), 0)
    m_i = lax.broadcasted_iota(jnp.int32, (samples, samples), 1)
    m_in = lax.rem(m_i, slots)
    s_of_m = (m_in // OWN) * (CORES * OWN) + (m_i // slots) * OWN + lax.rem(m_i, OWN)
    spread = jnp.where(s_i == s_of_m, 1.0, 0.0).astype(BF16)
    owner_rows = jnp.broadcast_to(osv[...].astype(F32), (16, samples)).astype(BF16)
    owner = jnp.dot(owner_rows, spread, preferred_element_type=F32)[0:1, :]
    i_i = lax.broadcasted_iota(jnp.int32, (slots, samples), 0)
    slot_i = (i_i // OWN) * (CORES * OWN) + c * OWN + lax.rem(i_i, OWN)
    pick = jnp.where(owner == slot_i.astype(F32), 1.0, 0.0).astype(BF16)

    many_q = qg.at[0, pl.ds(0, chips - 1)]
    remote(many_q, many_q, SQ, partner, y).wait_recv()
    swap_q = remote(qg.at[c], qg.at[c], SC, partner, y)
    swap_q.start()
    swap_q.wait_recv()

    qf32[...] = qg[...].reshape(samples * GROUP, WIDTH).astype(F32)
    by_head = jnp.concatenate(
        [qf32[pl.ds(h, samples, stride=GROUP), :].astype(BF16) for h in range(GROUP)], axis=1
    )
    picked = jnp.dot(pick, by_head, preferred_element_type=F32)
    for h in range(GROUP):
        qs32[pl.ds(h, slots, stride=GROUP), :] = picked[:, h * WIDTH : (h + 1) * WIDTH]

    load_k.wait()
    load_v.wait()
    swap_k.wait_recv()
    swap_v.wait_recv()
    swap_f.wait_recv()

    chunk_chips = 8
    chunk = chunk_chips * ROWS
    chunks = chips // chunk_chips
    row_in = lax.rem(lax.broadcasted_iota(jnp.int32, (chunk, WIDTH), 0), ROWS)
    lane = lax.broadcasted_iota(jnp.int32, (chunk, WIDTH), 1)

    def prompt_chunk(n):
        first = pl.multiple_of(n * chunk, chunk)
        qc = qs32[pl.ds(first, chunk), :].astype(BF16)
        parts = []
        for core in range(CORES):
            s = nt_dot(qc, kbuf[core])
            for b in range(blocks):
                parts.append(s[:, b * SPAN : (b + 1) * SPAN] * scb[core, b : b + 1, :])
        peak = functools.reduce(jnp.maximum, parts)
        peak = jnp.max(peak, axis=1, keepdims=True)
        parts = [jnp.exp2(s - peak) for s in parts]
        total = jnp.sum(functools.reduce(jnp.add, parts), axis=1, keepdims=True)
        numer = None
        for core in range(CORES):
            scaled = jnp.concatenate(
                [
                    (parts[core * blocks + b] * scb[core, blocks + b : blocks + b + 1, :]).astype(BF16)
                    for b in range(blocks)
                ],
                axis=1,
            )
            term = jnp.dot(scaled, vbuf[core], preferred_element_type=F32)
            numer = term if numer is None else numer + term
        nsend[pl.ds(first, chunk), :] = numer.astype(BF16)
        stats = jnp.where(lane == row_in, peak, 0.0) + jnp.where(lane == row_in + ROWS, total, 0.0)
        stats = jnp.sum(stats.reshape(chunk_chips, ROWS, WIDTH), axis=1)
        for i in range(chunk_chips):
            ssend[n * chunk_chips + i] = stats[i : i + 1, :]

    def send_partial(t):
        first = pl.multiple_of(t * ROWS, ROWS)
        remote(ssend.at[t], srecv.at[chip], SS, t * CORES + c, y).start()
        remote(nsend.at[pl.ds(first, ROWS)], nrecv.at[chip], SN, t * CORES + c, y).start()

    own_chunk = chip // chunk_chips

    def chunk_step(k, carry):
        off = lax.rem(k + chunks // 2, chunks)
        n = lax.rem(own_chunk + off, chunks)
        prompt_chunk(n)

        def send_one(i, inner):
            t = n * chunk_chips + i

            @pl.when(t != chip)
            def _():
                send_partial(t)

            return inner

        lax.fori_loop(0, chunk_chips, send_one, 0)
        return carry

    lax.fori_loop(0, chunks, chunk_step, 0)
    own_first = pl.multiple_of(chip * ROWS, ROWS)
    nrecv[chip] = nsend[pl.ds(own_first, ROWS), :]
    srecv[chip] = ssend[chip]

    load_sk.wait()
    load_sv.wait()
    load_sl.wait()
    own_q = qs32[pl.ds(own_first, ROWS), :].astype(BF16)
    limit = skb.shape[1]
    live_i = lax.broadcasted_iota(jnp.int32, (GROUP, limit), 1)
    near_numer, near_peak, near_total = [], [], []
    for j in range(OWN):
        live = live_i < sls[j]
        s = nt_dot(own_q, skb[j])[j * GROUP : (j + 1) * GROUP, :] * (WIDTH**-0.5 * LOG2E)
        s = jnp.where(live, s, NEG_FILL)
        peak = jnp.max(s, axis=1, keepdims=True)
        w = jnp.where(live, jnp.exp2(s - peak), 0.0)
        near_total.append(jnp.sum(w, axis=1, keepdims=True))
        near_peak.append(peak)
        w16 = jnp.concatenate([w, jnp.zeros_like(w)], axis=0).astype(BF16)
        near_numer.append(jnp.dot(w16, svb[j], preferred_element_type=F32)[:GROUP])
    near_numer = jnp.concatenate(near_numer, axis=0)
    near_peak = jnp.concatenate(near_peak, axis=0)
    near_total = jnp.concatenate(near_total, axis=0)

    many_s = srecv.at[pl.ds(0, chips - 1)]
    remote(many_s, many_s, SS, partner, y).wait_recv()
    stats = jnp.concatenate([srecv[i] for i in range(chips)], axis=0)
    stats = jnp.concatenate([stats, jnp.zeros((WIDTH - chips, WIDTH), F32)], axis=0)
    stats = jnp.transpose(stats)
    peaks = stats[0:ROWS, 0:chips]
    totals = stats[ROWS : 2 * ROWS, 0:chips]
    peak = jnp.maximum(jnp.max(peaks, axis=1, keepdims=True), near_peak)
    factor = jnp.exp2(peaks - peak)
    near_factor = jnp.exp2(near_peak - peak)
    total = jnp.sum(factor * totals, axis=1, keepdims=True) + near_total * near_factor
    many_n = nrecv.at[pl.ds(0, chips - 1)]
    remote(many_n, many_n, SN, partner, y).wait_recv()
    numer = near_numer * near_factor
    for i in range(chips):
        numer = numer + nrecv[i].astype(F32) * factor[:, i : i + 1]
    att[chip] = (numer / total).astype(BF16)

    def send_att(k, carry):
        t = lax.rem(chip + far_first(k), chips)
        remote(att.at[chip], att.at[chip], SA, t * CORES + c, y).start()
        return carry

    lax.fori_loop(1, chips, send_att, 0)
    load_w.wait()
    swap_w.wait_recv()
    many_a = att.at[pl.ds(0, chips - 1)]
    remote(many_a, many_a, SA, partner, y).wait_recv()

    a32[...] = att[...].reshape(slots * GROUP, WIDTH).astype(F32)
    rows = jnp.concatenate(
        [a32[pl.ds(h, slots, stride=GROUP), :].astype(BF16) for h in range(GROUP)], axis=1
    )
    per_group = slots // groups
    for core in range(CORES):
        part = jnp.dot(rows, wbuf[core], preferred_element_type=F32)
        ysend[core] = part.reshape(groups, per_group, part.shape[1])

    def send_out(k, carry):
        t = lax.rem(y + k, groups)
        remote(ysend.at[c, t], yrecv.at[c * groups + y], SY, chip * CORES + c, t).start()
        remote(ysend.at[other, t], yrecv.at[c * groups + y], SY, chip * CORES + other, t).start()
        return carry

    lax.fori_loop(1, groups, send_out, 0)
    remote(ysend.at[other, y], yrecv.at[c * groups + y], SY, partner, y).start()
    yrecv[c * groups + y] = ysend[c, y]
    many_y = yrecv.at[pl.ds(0, CORES * groups - 1)]
    last = remote(many_y, many_y, SY, partner, y)
    last.wait_recv()
    for core in range(CORES):
        acc = yrecv[core * groups]
        for i in range(1, groups):
            acc = acc + yrecv[core * groups + i]
        for q in range(per_group // OWN):
            first = q * CORES * OWN + core * OWN
            o_ref[first : first + OWN, :] = acc[q * OWN : (q + 1) * OWN, :]

    remote(many_q, many_q, SQ, partner, y).wait_send()
    swap_q.wait_send()
    swap_k.wait_send()
    swap_v.wait_send()
    swap_w.wait_send()
    swap_f.wait_send()
    remote(many_s, many_s, SS, partner, y).wait_send()
    remote(many_n, many_n, SN, partner, y).wait_send()
    remote(many_a, many_a, SA, partner, y).wait_send()
    last.wait_send()


def local(
    queries,
    owner_slot,
    suffix_len,
    prompt_keys,
    prompt_value_rows,
    key_scale,
    value_block_scale,
    suffix_key_rows,
    suffix_value_rows,
    out_weight,
):
    groups = lax.axis_size("kv")
    chips = lax.axis_size("seq") // CORES
    samples = chips * CORES * OWN
    slots = chips * OWN
    positions = prompt_keys.shape[0]
    blocks = key_scale.shape[0]
    limit = suffix_key_rows.shape[1]
    depth, columns = out_weight.shape
    out_rows = samples // groups
    any_spec = pl.BlockSpec(memory_space=pl.ANY)
    return pl.pallas_call(
        functools.partial(kernel, chips, groups),
        out_shape=jax.ShapeDtypeStruct((out_rows, columns), F32),
        in_specs=[any_spec] * 10,
        out_specs=pl.BlockSpec(memory_space=pltpu.VMEM),
        scratch_shapes=[
            pltpu.VMEM(queries.shape, BF16),
            pltpu.VMEM((1, samples), jnp.int32),
            pltpu.SMEM((OWN,), jnp.int32),
            pltpu.VMEM((CORES, positions, WIDTH), BF16),
            pltpu.VMEM((CORES, positions, WIDTH), BF16),
            pltpu.VMEM((blocks, 1), F32),
            pltpu.VMEM((blocks, 1), F32),
            pltpu.VMEM((CORES, 2 * blocks, WIDTH), F32),
            pltpu.VMEM((OWN, limit, WIDTH), BF16),
            pltpu.VMEM((OWN, limit, WIDTH), BF16),
            pltpu.VMEM((CORES, depth, columns), BF16),
            pltpu.VMEM((ROWS, WIDTH), F32),
            pltpu.VMEM((CORES, chips, ROWS, WIDTH), BF16),
            pltpu.VMEM((samples * GROUP, WIDTH), F32),
            pltpu.VMEM((slots * GROUP, WIDTH), F32),
            pltpu.VMEM((slots * GROUP, WIDTH), BF16),
            pltpu.VMEM((chips, 1, WIDTH), F32),
            pltpu.VMEM((chips, ROWS, WIDTH), BF16),
            pltpu.VMEM((chips, 1, WIDTH), F32),
            pltpu.VMEM((chips, ROWS, WIDTH), BF16),
            pltpu.VMEM((slots * GROUP, WIDTH), F32),
            pltpu.VMEM((CORES, groups, slots // groups, columns), F32),
            pltpu.VMEM((CORES * groups, slots // groups, columns), F32),
            pltpu.SemaphoreType.DMA((10,)),
            pltpu.SemaphoreType.DMA((10,)),
            pltpu.SemaphoreType.DMA((10,)),
        ],
        compiler_params=pltpu.CompilerParams(
            collective_id=0, has_side_effects=True, vmem_limit_bytes=32 * 1024 * 1024
        ),
        name="decode_attention",
    )(
        queries,
        owner_slot.reshape(1, samples),
        suffix_len,
        prompt_keys,
        prompt_value_rows,
        key_scale,
        value_block_scale,
        suffix_key_rows,
        suffix_value_rows,
        out_weight,
    )


def solution(mesh):
    in_specs = (
        P("seq", "kv"),
        P(),
        P("seq"),
        P("seq", "kv"),
        P("seq", "kv"),
        P("seq", "kv"),
        P("seq", "kv"),
        P("seq", None, "kv"),
        P("seq", None, "kv"),
        P("kv", "seq"),
    )
    out_specs = P("kv", "seq")
    return jax.shard_map(local, mesh=mesh, in_specs=in_specs, out_specs=out_specs, check_vma=False)
```

time: 208 us -> 49.3 us (0.24)
  the two profiles are of different devices: /device:TPU:2 before, /device:TPU:1 now
where the time goes in v1:
time: 49.3 us; the launch traced here: 49.1 us
  Pallas kernels  45 us (91%)
  local copies, waits for them, and re-layouts  4.06 us (8%)
    pallas_call x1, Pallas kernels, local(): pl.pallas_call(functools.partial(kernel, chips, groups), out_shape=jax.Sh...  45 us
    unnamed x22, local copies, waits for them, and re-layouts  4.06 us

profile of v1, /device:TPU:1, one launch (start us, length us, event | category | flops | bytes accessed | tf_op | source)
XLA Modules:
  0.0 49.1 jit_solution(11834497010343588207)
XLA Ops:
  0.0 0.0 copy-start.7
  0.0 0.7 %copy-done.7 = f32[4,1]{0,1:T(1,128)S(1)} copy-done((f32[4,1]{0,1:T(1,128)S(1)}, f32[4,1]{0,1:T(1,128)}, u32[]{:S(2)}) %copy-start.7) | copy-done | bytes 40
  0.7 0.0 copy-start.8
  0.7 0.1 copy.11.ks_hbm
  0.8 0.6 %copy-done.8 = f32[4,1]{0,1:T(1,128)S(1)} copy-done((f32[4,1]{0,1:T(1,128)S(1)}, f32[4,1]{0,1:T(1,128)}, u32[]{:S(2)}) %copy-start.8) | copy-done | bytes 40
  1.3 0.1 copy.12.vs_hbm
  1.4 0.0 copy-start
  1.4 0.0 copy-start.1
  1.4 0.0 copy-start.2
  1.4 0.0 copy-start.4
  1.4 0.0 copy-start.5
  1.4 0.0 copy-start.6
  1.4 1.1 %copy.13.w_hbm = bf16[1024,80]{1,0:T(8,128)(2,1)S(1)} copy(bf16[1024,80]{0,1:T(8,128)(2,1)} %param.19) | data formatting | bytes 327680 | tf_op args[9]
  2.6 0.0 copy-done
  2.6 0.0 copy-done.1
  2.6 0.0 copy-done.2
  2.6 0.0 copy-done.4
  2.6 0.0 copy-done.5
  2.6 0.0 copy-done.6
  2.6 0.0 copy-start.3
  2.7 0.9 %copy-done.3 = bf16[2,256,128]{2,1,0:T(8,128)(2,1)S(1)} copy-done((bf16[2,256,128]{2,1,0:T(8,128)(2,1)S(1)}, bf16[2,256,128]{2,1,0:T(8,128)(2,1)}, u32[]{:S(2)}) %copy-start.3) | copy-done | bytes 131096
  3.5 45.0 %decode_attention.1 = f32[16,80]{1,0:T(8,128)S(1)} custom-call(bf16[2,1024]{1,0:T(2,128)(2,1)S(1)} %copy-done.4, s32[1,128]{1,0:T(1,128)S(1)} %bitcast.1, s32[2]{0:T(128)S(1)} %copy-done.6, bf16[512,128]{1,0:T(8,128)(2,1)S(1)} %copy-done, bf16[512,128]{1,0:T(8,128)(2,1)S(1)} %copy-done.1, f32[4,1]{1,0:T(4,128)S(1)} %copy.11.ks_hbm, f32[4,1]{1,0:T(4,128)S(1)} %copy.12.vs_hbm, ...), custom_call_target="tpu_custom_call" | custom-call | tf_op jit(solution)/shard_map/decode_attention/pallas_call | solution.py:371
  48.5 0.6 %copy.15 = f32[16,80]{1,0:T(8,128)} copy(f32[16,80]{1,0:T(8,128)S(1)} %decode_attention.1) | data formatting | bytes 10240
Async XLA Ops:
  0.0 0.7 %copy-start.7 = (f32[4,1]{0,1:T(1,128)S(1)}, f32[4,1]{0,1:T(1,128)}, u32[]{:S(2)}) copy-start(f32[4,1]{0,1:T(1,128)} %param.15) | copy-start | bytes 52
  0.7 0.7 %copy-start.8 = (f32[4,1]{0,1:T(1,128)S(1)}, f32[4,1]{0,1:T(1,128)}, u32[]{:S(2)}) copy-start(f32[4,1]{0,1:T(1,128)} %param.16) | copy-start | bytes 52
  1.4 1.2 %copy-start = (bf16[512,128]{1,0:T(8,128)(2,1)S(1)}, bf16[512,128]{1,0:T(8,128)(2,1)}, u32[]{:S(2)}) copy-start(bf16[512,128]{1,0:T(8,128)(2,1)} %k_hbm.1) | copy-start | bytes 393220
  1.4 1.2 %copy-start.1 = (bf16[512,128]{1,0:T(8,128)(2,1)S(1)}, bf16[512,128]{1,0:T(8,128)(2,1)}, u32[]{:S(2)}) copy-start(bf16[512,128]{1,0:T(8,128)(2,1)} %v_hbm.1) | copy-start | bytes 393220
  1.4 1.2 %copy-start.2 = (bf16[2,256,128]{2,1,0:T(8,128)(2,1)S(1)}, bf16[2,256,128]{2,1,0:T(8,128)(2,1)}, u32[]{:S(2)}) copy-start(bf16[2,256,128]{2,1,0:T(8,128)(2,1)} %sk_hbm.1) | copy-start | bytes 393220
  1.4 1.2 %copy-start.4 = (bf16[2,1024]{1,0:T(2,128)(2,1)S(1)}, bf16[2,1024]{1,0:T(2,128)(2,1)}, u32[]{:S(2)}) copy-start(bf16[2,1024]{1,0:T(2,128)(2,1)} %q_hbm.1) | copy-start | bytes 12292
  1.4 1.2 %copy-start.5 = (s32[128]{0:T(128)S(1)}, s32[128]{0:T(128)}, u32[]{:S(2)}) copy-start(s32[128]{0:T(128)} %param.11) | copy-start | bytes 1540
  1.4 1.2 %copy-start.6 = (s32[2]{0:T(128)S(1)}, s32[2]{0:T(128)}, u32[]{:S(2)}) copy-start(s32[2]{0:T(128)} %sl_hbm.1) | copy-start | bytes 28
  2.6 0.9 %copy-start.3 = (bf16[2,256,128]{2,1,0:T(8,128)(2,1)S(1)}, bf16[2,256,128]{2,1,0:T(8,128)(2,1)}, u32[]{:S(2)}) copy-start(bf16[2,256,128]{2,1,0:T(8,128)(2,1)} %sv_hbm.1) | copy-start | bytes 393220

commit v2 on v1

--- a/solution.py
+++ b/solution.py
@@ -14,6 +14,7 @@
 NEG_FILL = -1e30
 
 CORES = 2
+ROW_CHIPS = 4
 GROUP = 8
 WIDTH = 128
 OWN = 2
@@ -74,6 +75,7 @@
     c = lax.rem(me, CORES)
     chip = me // CORES
     other = 1 - c
+    depth_chips = chips // ROW_CHIPS
 
     def load(src, dst, i):
         cp = pltpu.make_async_copy(src, dst, lsem.at[i])
@@ -91,6 +93,38 @@
         )
 
     load_q = load(q_hbm, qown, LQ)
+
+    def far_first(k):
+        a, b = k // ROW_CHIPS, lax.rem(k, ROW_CHIPS)
+        return lax.rem(chip // ROW_CHIPS + far_offset(a, depth_chips), depth_chips) * ROW_CHIPS + far_in_row(b)
+
+    def far_in_row(b):
+        return lax.rem(chip + far_offset(b, ROW_CHIPS), ROW_CHIPS)
+
+    def far_offset(k, size):
+        step = jnp.where(lax.rem(k, 2) == 0, size // 2 - k // 2, size // 2 + (k + 1) // 2)
+        return jnp.where(k == size - 1, 0, step)
+
+    barrier = pltpu.get_barrier_semaphore()
+
+    def greet(seq, kv):
+        pl.semaphore_signal(barrier, inc=1, device_id={"kv": kv, "seq": seq}, device_id_type=MESH)
+
+    def greet_plane(k, carry):
+        greet(far_first(k) * CORES + c, y)
+        return carry
+
+    lax.fori_loop(0, chips - 1, greet_plane, 0, unroll=True)
+
+    def greet_column(k, carry):
+        kv = lax.rem(y + far_offset(k, groups), groups)
+        greet(chip * CORES + c, kv)
+        greet(chip * CORES + other, kv)
+        return carry
+
+    lax.fori_loop(0, groups - 1, greet_column, 0, unroll=True)
+    greet(chip * CORES + other, y)
+
     load_o = load(os_hbm, osv, LO)
     load_ks = load(ks_hbm, ksv, LKS)
     load_vs = load(vs_hbm, vsv, LVS)
@@ -101,25 +135,6 @@
     load_sv = load(sv_hbm, svb, LSV)
     load_sl = load(sl_hbm, sls, LSL)
 
-    barrier = pltpu.get_barrier_semaphore()
-
-    def greet(seq, kv):
-        pl.semaphore_signal(barrier, inc=1, device_id={"kv": kv, "seq": seq}, device_id_type=MESH)
-
-    def greet_plane(k, carry):
-        greet(lax.rem(chip + k, chips) * CORES + c, y)
-        return carry
-
-    lax.fori_loop(1, chips, greet_plane, 0)
-
-    def greet_column(k, carry):
-        greet(chip * CORES + c, lax.rem(y + k, groups))
-        greet(chip * CORES + other, lax.rem(y + k, groups))
-        return carry
-
-    lax.fori_loop(1, groups, greet_column, 0)
-    greet(chip * CORES + other, y)
-
     load_q.wait()
     for h in range(GROUP):
         piece = qown[:, h * WIDTH : (h + 1) * WIDTH].astype(F32)
@@ -129,18 +144,11 @@
 
     pl.semaphore_wait(barrier, (chips - 1) + 2 * (groups - 1) + 1)
 
-    half = chips // 2
-
-    def far_first(k):
-        step = half - (k // 2)
-        return lax.rem(jnp.where(lax.rem(k, 2) == 0, step, chips - step), chips)
-
     def send_queries(k, carry):
-        t = lax.rem(chip + far_first(k), chips)
-        remote(qg.at[c, chip], qg.at[c, chip], SQ, t * CORES + c, y).start()
-        return carry
-
-    lax.fori_loop(1, chips, send_queries, 0)
+        remote(qg.at[c, chip], qg.at[c, chip], SQ, far_first(k) * CORES + c, y).start()
+        return carry
+
+    lax.fori_loop(0, chips - 1, send_queries, 0, unroll=True)
 
     partner = chip * CORES + other
     swap_k = remote(k_hbm, kbuf.at[c], SK, partner, y)
@@ -151,9 +159,13 @@
     swap_w.start()
     load_ks.wait()
     load_vs.wait()
-    blocks = ksv.shape[0]
-    scb[c, 0:blocks, :] = jnp.broadcast_to(ksv[...] * (WIDTH**-0.5 * LOG2E), (blocks, WIDTH))
-    scb[c, blocks : 2 * blocks, :] = jnp.broadcast_to(vsv[...], (blocks, WIDTH))
+    blocks = ksv.shape[1]
+    scb[c, 0:blocks, :] = jnp.concatenate(
+        [jnp.broadcast_to(ksv[:, b : b + 1] * (WIDTH**-0.5 * LOG2E), (1, WIDTH)) for b in range(blocks)], axis=0
+    )
+    scb[c, blocks : 2 * blocks, :] = jnp.concatenate(
+        [jnp.broadcast_to(vsv[:, b : b + 1], (1, WIDTH)) for b in range(blocks)], axis=0
+    )
     swap_f = remote(scb.at[c], scb.at[c], SF, partner, y)
     swap_f.start()
 
@@ -239,7 +251,7 @@
         prompt_chunk(n)
 
         def send_one(i, inner):
-            t = n * chunk_chips + i
+            t = n * chunk_chips + (i // ROW_CHIPS) * ROW_CHIPS + far_in_row(lax.rem(i, ROW_CHIPS))
 
             @pl.when(t != chip)
             def _():
@@ -247,7 +259,7 @@
 
             return inner
 
-        lax.fori_loop(0, chunk_chips, send_one, 0)
+        lax.fori_loop(0, chunk_chips, send_one, 0, unroll=True)
         return carry
 
     lax.fori_loop(0, chunks, chunk_step, 0)
@@ -295,11 +307,10 @@
     att[chip] = (numer / total).astype(BF16)
 
     def send_att(k, carry):
-        t = lax.rem(chip + far_first(k), chips)
-        remote(att.at[chip], att.at[chip], SA, t * CORES + c, y).start()
-        return carry
-
-    lax.fori_loop(1, chips, send_att, 0)
+        remote(att.at[chip], att.at[chip], SA, far_first(k) * CORES + c, y).start()
+        return carry
+
+    lax.fori_loop(0, chips - 1, send_att, 0, unroll=True)
     load_w.wait()
     swap_w.wait_recv()
     many_a = att.at[pl.ds(0, chips - 1)]
@@ -311,16 +322,16 @@
     )
     per_group = slots // groups
     for core in range(CORES):
-        part = jnp.dot(rows, wbuf[core], preferred_element_type=F32)
+        part = nt_dot(rows, wbuf[core])
         ysend[core] = part.reshape(groups, per_group, part.shape[1])
 
     def send_out(k, carry):
-        t = lax.rem(y + k, groups)
+        t = lax.rem(y + far_offset(k, groups), groups)
         remote(ysend.at[c, t], yrecv.at[c * groups + y], SY, chip * CORES + c, t).start()
         remote(ysend.at[other, t], yrecv.at[c * groups + y], SY, chip * CORES + other, t).start()
         return carry
 
-    lax.fori_loop(1, groups, send_out, 0)
+    lax.fori_loop(0, groups - 1, send_out, 0, unroll=True)
     remote(ysend.at[other, y], yrecv.at[c * groups + y], SY, partner, y).start()
     yrecv[c * groups + y] = ysend[c, y]
     many_y = yrecv.at[pl.ds(0, CORES * groups - 1)]
@@ -379,12 +390,12 @@
             pltpu.SMEM((OWN,), jnp.int32),
             pltpu.VMEM((CORES, positions, WIDTH), BF16),
             pltpu.VMEM((CORES, positions, WIDTH), BF16),
-            pltpu.VMEM((blocks, 1), F32),
-            pltpu.VMEM((blocks, 1), F32),
+            pltpu.VMEM((1, blocks), F32),
+            pltpu.VMEM((1, blocks), F32),
             pltpu.VMEM((CORES, 2 * blocks, WIDTH), F32),
             pltpu.VMEM((OWN, limit, WIDTH), BF16),
             pltpu.VMEM((OWN, limit, WIDTH), BF16),
-            pltpu.VMEM((CORES, depth, columns), BF16),
+            pltpu.VMEM((CORES, columns, depth), BF16),
             pltpu.VMEM((ROWS, WIDTH), F32),
             pltpu.VMEM((CORES, chips, ROWS, WIDTH), BF16),
             pltpu.VMEM((samples * GROUP, WIDTH), F32),
@@ -402,7 +413,7 @@
             pltpu.SemaphoreType.DMA((10,)),
         ],
         compiler_params=pltpu.CompilerParams(
-            collective_id=0, has_side_effects=True, vmem_limit_bytes=32 * 1024 * 1024
+            collective_id=0, has_side_effects=True, vmem_limit_bytes=56508416
         ),
         name="decode_attention",
     )(
@@ -411,11 +422,11 @@
         suffix_len,
         prompt_keys,
         prompt_value_rows,
-        key_scale,
-        value_block_scale,
+        key_scale.reshape(1, blocks),
+        value_block_scale.reshape(1, blocks),
         suffix_key_rows,
         suffix_value_rows,
-        out_weight,
+        out_weight.T,
     )
 
 

time: 49.3 us -> 44.3 us (0.90)
  local copies, waits for them, and re-layouts: 4.06 us -> 1.3 us
  Pallas kernels: 45 us -> 42.8 us
    unnamed x22 -> x11, local copies, waits for them, and re-layouts: 4.06 us -> 1.3 us
    pallas_call x1, Pallas kernels: 45 us -> 42.8 us  [local(): pl.pallas_call(functools.partial(kernel, chips, groups), out_shape=jax.Sh...]
where the time goes in v2:
time: 44.3 us; the launch traced here: 44.2 us
  Pallas kernels  42.8 us (97%)
  local copies, waits for them, and re-layouts  1.3 us (3%)
    pallas_call x1, Pallas kernels, local(): pl.pallas_call(functools.partial(kernel, chips, groups), out_shape=jax.Sh...  42.8 us
    unnamed x11, local copies, waits for them, and re-layouts  1.3 us

profile of v2, /device:TPU:1, one launch (start us, length us, event | category | flops | bytes accessed | tf_op | source)
XLA Modules:
  0.0 44.2 jit_solution(12291451380602662812)
XLA Ops:
  0.0 0.0 copy-start
  0.0 0.0 copy-start.4
  0.0 0.0 copy-start.1
  0.0 0.0 copy-start.2
  0.0 0.0 copy-start.3
  0.0 0.7 %copy-done = bf16[2,1024]{1,0:T(2,128)(2,1)S(1)} copy-done((bf16[2,1024]{1,0:T(2,128)(2,1)S(1)}, bf16[2,1024]{1,0:T(2,128)(2,1)}, u32[]{:S(2)}) %copy-start) | copy-done | bytes 4120
  0.7 0.0 copy-done.4
  0.7 0.0 copy-done.1
  0.7 0.0 copy-done.2
  0.7 0.0 copy-done.3
  0.7 42.8 %decode_attention.1 = f32[16,80]{1,0:T(8,128)S(1)} custom-call(bf16[2,1024]{1,0:T(2,128)(2,1)S(1)} %copy-done, s32[1,128]{1,0:T(1,128)S(1)} %bitcast.4, s32[2]{0:T(128)S(1)} %copy-done.2, bf16[512,128]{1,0:T(8,128)(2,1)} %k_hbm.1, bf16[512,128]{1,0:T(8,128)(2,1)} %v_hbm.1, f32[1,4]{1,0:T(1,128)S(1)} %bitcast.5, f32[1,4]{1,0:T(1,128)S(1)} %bitcast.6, ...), custom_call_target="tpu_custom_call" | custom-call | tf_op jit(solution)/shard_map/decode_attention/pallas_call | solution.py:382
  43.5 0.6 %copy.12 = f32[16,80]{1,0:T(8,128)} copy(f32[16,80]{1,0:T(8,128)S(1)} %decode_attention.1) | data formatting | bytes 10240
Async XLA Ops:
  0.0 0.7 %copy-start = (bf16[2,1024]{1,0:T(2,128)(2,1)S(1)}, bf16[2,1024]{1,0:T(2,128)(2,1)}, u32[]{:S(2)}) copy-start(bf16[2,1024]{1,0:T(2,128)(2,1)} %q_hbm.1) | copy-start | bytes 12292
  0.0 0.7 %copy-start.4 = (f32[4,1]{0,1:T(1,128)S(1)}, f32[4,1]{0,1:T(1,128)}, u32[]{:S(2)}) copy-start(f32[4,1]{0,1:T(1,128)} %param.16) | copy-start | bytes 52
  0.0 0.7 %copy-start.1 = (s32[128]{0:T(128)S(1)}, s32[128]{0:T(128)}, u32[]{:S(2)}) copy-start(s32[128]{0:T(128)} %param.11) | copy-start | bytes 1540
  0.0 0.7 %copy-start.2 = (s32[2]{0:T(128)S(1)}, s32[2]{0:T(128)}, u32[]{:S(2)}) copy-start(s32[2]{0:T(128)} %sl_hbm.1) | copy-start | bytes 28
  0.0 0.7 %copy-start.3 = (f32[4,1]{0,1:T(1,128)S(1)}, f32[4,1]{0,1:T(1,128)}, u32[]{:S(2)}) copy-start(f32[4,1]{0,1:T(1,128)} %param.15) | copy-start | bytes 52

commit v3 on v2

--- a/solution.py
+++ b/solution.py
@@ -381,7 +381,7 @@
     any_spec = pl.BlockSpec(memory_space=pl.ANY)
     return pl.pallas_call(
         functools.partial(kernel, chips, groups),
-        out_shape=jax.ShapeDtypeStruct((out_rows, columns), F32),
+        out_shape=pltpu.VMEM((out_rows, columns), F32),
         in_specs=[any_spec] * 10,
         out_specs=pl.BlockSpec(memory_space=pltpu.VMEM),
         scratch_shapes=[
@@ -413,7 +413,7 @@
             pltpu.SemaphoreType.DMA((10,)),
         ],
         compiler_params=pltpu.CompilerParams(
-            collective_id=0, has_side_effects=True, vmem_limit_bytes=56508416
+            collective_id=0, has_side_effects=True, vmem_limit_bytes=60 * 1024 * 1024
         ),
         name="decode_attention",
     )(

time: 44.3 us -> 43.6 us (0.984)
  local copies, waits for them, and re-layouts: 1.3 us -> 0.6 us
    unnamed x11 -> x1, local copies, waits for them, and re-layouts: 1.3 us -> 0.6 us
where the time goes in v3:
time: 43.6 us; the launch traced here: 43.4 us
  Pallas kernels  42.8 us (98%)
  local copies, waits for them, and re-layouts  0.6 us (1%)
    pallas_call x1, Pallas kernels, local(): pl.pallas_call(functools.partial(kernel, chips, groups), out_shape=pltpu....  42.8 us

profile of v3, /device:TPU:1, one launch (start us, length us, event | category | flops | bytes accessed | tf_op | source)
XLA Modules:
  0.0 43.4 jit_solution(12310970666353919384)
XLA Ops:
  0.0 42.8 %decode_attention.1 = f32[16,80]{1,0:T(8,128)S(1)} custom-call(bf16[2,1024]{1,0:T(2,128)(2,1)} %q_hbm.1, s32[1,128]{1,0:T(1,128)} %bitcast.5, s32[2]{0:T(128)} %sl_hbm.1, bf16[512,128]{1,0:T(8,128)(2,1)} %k_hbm.1, bf16[512,128]{1,0:T(8,128)(2,1)} %v_hbm.1, f32[1,4]{1,0:T(1,128)} %bitcast.6, f32[1,4]{1,0:T(1,128)} %bitcast.7, bf16[2,256,128]{2,1,0:T(8,128)(2,1)} %sk_hbm.1, ...), custom_call_target="tpu_custom_call" | custom-call | tf_op jit(solution)/shard_map/decode_attention/pallas_call | solution.py:382
  42.8 0.6 %copy.12 = f32[16,80]{1,0:T(8,128)} copy(f32[16,80]{1,0:T(8,128)S(1)} %decode_attention.1) | data formatting | bytes 10240

commit v4 on v3

--- a/solution.py
+++ b/solution.py
@@ -27,6 +27,10 @@
 
 def nt_dot(a, b):
     return lax.dot_general(a, b, (((1,), (1,)), ((), ())), preferred_element_type=F32)
+
+
+def near_first(size):
+    return [0] + [k for step in range(1, size // 2) for k in (step, size - step)] + [size // 2]
 
 
 def kernel(
@@ -69,6 +73,7 @@
     ssem,
     rsem,
     lsem,
+    asem,
 ):
     me = lax.axis_index("seq")
     y = lax.axis_index("kv")
@@ -307,33 +312,49 @@
     att[chip] = (numer / total).astype(BF16)
 
     def send_att(k, carry):
-        remote(att.at[chip], att.at[chip], SA, far_first(k) * CORES + c, y).start()
+        pltpu.make_async_remote_copy(
+            src_ref=att.at[chip],
+            dst_ref=att.at[chip],
+            send_sem=ssem.at[SA],
+            recv_sem=asem.at[far_offset(k // ROW_CHIPS, depth_chips)],
+            device_id={"kv": y, "seq": far_first(k) * CORES + c},
+            device_id_type=MESH,
+        ).start()
         return carry
 
     lax.fori_loop(0, chips - 1, send_att, 0, unroll=True)
     load_w.wait()
     swap_w.wait_recv()
-    many_a = att.at[pl.ds(0, chips - 1)]
-    remote(many_a, many_a, SA, partner, y).wait_recv()
-
-    a32[...] = att[...].reshape(slots * GROUP, WIDTH).astype(F32)
-    rows = jnp.concatenate(
-        [a32[pl.ds(h, slots, stride=GROUP), :].astype(BF16) for h in range(GROUP)], axis=1
-    )
-    per_group = slots // groups
-    for core in range(CORES):
-        part = nt_dot(rows, wbuf[core])
-        ysend[core] = part.reshape(groups, per_group, part.shape[1])
-
-    def send_out(k, carry):
-        t = lax.rem(y + far_offset(k, groups), groups)
-        remote(ysend.at[c, t], yrecv.at[c * groups + y], SY, chip * CORES + c, t).start()
-        remote(ysend.at[other, t], yrecv.at[c * groups + y], SY, chip * CORES + other, t).start()
-        return carry
-
-    lax.fori_loop(0, groups - 1, send_out, 0, unroll=True)
-    remote(ysend.at[other, y], yrecv.at[c * groups + y], SY, partner, y).start()
-    yrecv[c * groups + y] = ysend[c, y]
+    row = chip // ROW_CHIPS
+    per_group = ROW_CHIPS * OWN
+    for n, k in enumerate(near_first(depth_chips)):
+        t = lax.rem(row + depth_chips - k, depth_chips)
+        arrived = att.at[pl.ds(0, ROW_CHIPS - (k == 0))]
+        pltpu.make_async_remote_copy(
+            src_ref=arrived,
+            dst_ref=arrived,
+            send_sem=ssem.at[SA],
+            recv_sem=asem.at[k],
+            device_id={"kv": y, "seq": partner},
+            device_id_type=MESH,
+        ).wait_recv()
+        first = pl.multiple_of(t * ROW_CHIPS, ROW_CHIPS)
+        a32[n] = att[pl.ds(first, ROW_CHIPS)].reshape(per_group * GROUP, WIDTH).astype(F32)
+        rows = jnp.concatenate(
+            [a32[n, pl.ds(h, per_group, stride=GROUP), :].astype(BF16) for h in range(GROUP)], axis=1
+        )
+        for core in range(CORES):
+            ysend[core, n] = nt_dot(rows, wbuf[core])
+        remote(ysend.at[other, n], yrecv.at[c * groups + y], SY, chip * CORES + other, t).start()
+
+        @pl.when(t != y)
+        def _():
+            remote(ysend.at[c, n], yrecv.at[c * groups + y], SY, chip * CORES + c, t).start()
+
+        @pl.when(t == y)
+        def _():
+            yrecv[c * groups + y] = ysend[c, n]
+
     many_y = yrecv.at[pl.ds(0, CORES * groups - 1)]
     last = remote(many_y, many_y, SY, partner, y)
     last.wait_recv()
@@ -353,6 +374,7 @@
     swap_f.wait_send()
     remote(many_s, many_s, SS, partner, y).wait_send()
     remote(many_n, many_n, SN, partner, y).wait_send()
+    many_a = att.at[pl.ds(0, chips - 1)]
     remote(many_a, many_a, SA, partner, y).wait_send()
     last.wait_send()
 
@@ -405,12 +427,13 @@
             pltpu.VMEM((chips, ROWS, WIDTH), BF16),
             pltpu.VMEM((chips, 1, WIDTH), F32),
             pltpu.VMEM((chips, ROWS, WIDTH), BF16),
-            pltpu.VMEM((slots * GROUP, WIDTH), F32),
+            pltpu.VMEM((groups, slots // groups * GROUP, WIDTH), F32),
             pltpu.VMEM((CORES, groups, slots // groups, columns), F32),
             pltpu.VMEM((CORES * groups, slots // groups, columns), F32),
             pltpu.SemaphoreType.DMA((10,)),
             pltpu.SemaphoreType.DMA((10,)),
             pltpu.SemaphoreType.DMA((10,)),
+            pltpu.SemaphoreType.DMA((chips // ROW_CHIPS,)),
         ],
         compiler_params=pltpu.CompilerParams(
             collective_id=0, has_side_effects=True, vmem_limit_bytes=60 * 1024 * 1024

time: 43.6 us -> 42 us (0.963)
  the two profiles are of different devices: /device:TPU:1 before, /device:TPU:9 now
where the time goes in v4:
time: 42 us; the launch traced here: 41.9 us
  Pallas kernels  41.3 us (98%)
  local copies, waits for them, and re-layouts  0.6 us (1%)
    pallas_call x1, Pallas kernels, local(): pl.pallas_call(functools.partial(kernel, chips, groups), out_shape=pltpu....  41.3 us

profile of v4, /device:TPU:9, one launch (start us, length us, event | category | flops | bytes accessed | tf_op | source)
XLA Modules:
  0.0 41.9 jit_solution(11675393228350947337)
XLA Ops:
  0.0 41.3 %decode_attention.1 = f32[16,80]{1,0:T(8,128)S(1)} custom-call(bf16[2,1024]{1,0:T(2,128)(2,1)} %q_hbm.1, s32[1,128]{1,0:T(1,128)} %bitcast.5, s32[2]{0:T(128)} %sl_hbm.1, bf16[512,128]{1,0:T(8,128)(2,1)} %k_hbm.1, bf16[512,128]{1,0:T(8,128)(2,1)} %v_hbm.1, f32[1,4]{1,0:T(1,128)} %bitcast.6, f32[1,4]{1,0:T(1,128)} %bitcast.7, bf16[2,256,128]{2,1,0:T(8,128)(2,1)} %sk_hbm.1, ...), custom_call_target="tpu_custom_call" | custom-call | tf_op jit(solution)/shard_map/decode_attention/pallas_call | solution.py:404
  41.3 0.6 %copy.12 = f32[16,80]{1,0:T(8,128)} copy(f32[16,80]{1,0:T(8,128)S(1)} %decode_attention.1) | data formatting | bytes 10240

commit v5 on v4

--- a/solution.py
+++ b/solution.py
@@ -29,8 +29,10 @@
     return lax.dot_general(a, b, (((1,), (1,)), ((), ())), preferred_element_type=F32)
 
 
-def near_first(size):
-    return [0] + [k for step in range(1, size // 2) for k in (step, size - step)] + [size // 2]
+def near_pairs(size):
+    pairs = [[0]] + [[step, size - step] for step in range(1, size // 2)] + [[size // 2]]
+    places = iter(range(size))
+    return [[(next(places), k) for k in pair] for pair in pairs]
 
 
 def kernel(
@@ -311,49 +313,63 @@
         numer = numer + nrecv[i].astype(F32) * factor[:, i : i + 1]
     att[chip] = (numer / total).astype(BF16)
 
-    def send_att(k, carry):
+    row = chip // ROW_CHIPS
+
+    def send_att(to, t):
         pltpu.make_async_remote_copy(
             src_ref=att.at[chip],
             dst_ref=att.at[chip],
             send_sem=ssem.at[SA],
-            recv_sem=asem.at[far_offset(k // ROW_CHIPS, depth_chips)],
-            device_id={"kv": y, "seq": far_first(k) * CORES + c},
+            recv_sem=asem.at[lax.rem(to - row + depth_chips, depth_chips)],
+            device_id={"kv": y, "seq": t * CORES + c},
             device_id_type=MESH,
         ).start()
-        return carry
-
-    lax.fori_loop(0, chips - 1, send_att, 0, unroll=True)
+
+    for to in range(depth_chips):
+        for b in range(ROW_CHIPS):
+            t = to * ROW_CHIPS + far_in_row(b)
+            if b < ROW_CHIPS - 1:
+                send_att(to, t)
+            else:
+                pl.when(t != chip)(functools.partial(send_att, to, t))
     load_w.wait()
     swap_w.wait_recv()
-    row = chip // ROW_CHIPS
     per_group = ROW_CHIPS * OWN
-    for n, k in enumerate(near_first(depth_chips)):
-        t = lax.rem(row + depth_chips - k, depth_chips)
-        arrived = att.at[pl.ds(0, ROW_CHIPS - (k == 0))]
-        pltpu.make_async_remote_copy(
-            src_ref=arrived,
-            dst_ref=arrived,
-            send_sem=ssem.at[SA],
-            recv_sem=asem.at[k],
-            device_id={"kv": y, "seq": partner},
-            device_id_type=MESH,
-        ).wait_recv()
-        first = pl.multiple_of(t * ROW_CHIPS, ROW_CHIPS)
-        a32[n] = att[pl.ds(first, ROW_CHIPS)].reshape(per_group * GROUP, WIDTH).astype(F32)
+    for pair in near_pairs(depth_chips):
+        ts = [lax.rem(row + depth_chips - k, depth_chips) for _, k in pair]
+        for (n, k), t in zip(pair, ts):
+            arrived = att.at[pl.ds(0, ROW_CHIPS - (k == 0))]
+            pltpu.make_async_remote_copy(
+                src_ref=arrived,
+                dst_ref=arrived,
+                send_sem=ssem.at[SA],
+                recv_sem=asem.at[k],
+                device_id={"kv": y, "seq": partner},
+                device_id_type=MESH,
+            ).wait_recv()
+            first = pl.multiple_of(t * ROW_CHIPS, ROW_CHIPS)
+            a32[n] = att[pl.ds(first, ROW_CHIPS)].reshape(per_group * GROUP, WIDTH).astype(F32)
         rows = jnp.concatenate(
-            [a32[n, pl.ds(h, per_group, stride=GROUP), :].astype(BF16) for h in range(GROUP)], axis=1
+            [
+                jnp.concatenate([a32[n, pl.ds(h, per_group, stride=GROUP), :] for n, _ in pair], axis=0).astype(BF16)
+                for h in range(GROUP)
+            ],
+            axis=1,
         )
         for core in range(CORES):
-            ysend[core, n] = nt_dot(rows, wbuf[core])
-        remote(ysend.at[other, n], yrecv.at[c * groups + y], SY, chip * CORES + other, t).start()
-
-        @pl.when(t != y)
-        def _():
-            remote(ysend.at[c, n], yrecv.at[c * groups + y], SY, chip * CORES + c, t).start()
-
-        @pl.when(t == y)
-        def _():
-            yrecv[c * groups + y] = ysend[c, n]
+            part = nt_dot(rows, wbuf[core])
+            for m, (n, _) in enumerate(pair):
+                ysend[core, n] = part[m * per_group : (m + 1) * per_group, :]
+        for (n, _), t in zip(pair, ts):
+            remote(ysend.at[other, n], yrecv.at[c * groups + y], SY, chip * CORES + other, t).start()
+
+            @pl.when(t != y)
+            def _():
+                remote(ysend.at[c, n], yrecv.at[c * groups + y], SY, chip * CORES + c, t).start()
+
+            @pl.when(t == y)
+            def _():
+                yrecv[c * groups + y] = ysend[c, n]
 
     many_y = yrecv.at[pl.ds(0, CORES * groups - 1)]
     last = remote(many_y, many_y, SY, partner, y)

time: 42 us -> 41.1 us (0.979)
  the two profiles are of different devices: /device:TPU:9 before, /device:TPU:8 now
where the time goes in v5:
time: 41.1 us; the launch traced here: 41 us
  Pallas kernels  40.4 us (98%)
  local copies, waits for them, and re-layouts  0.6 us (1%)
    pallas_call x1, Pallas kernels, local(): pl.pallas_call(functools.partial(kernel, chips, groups), out_shape=pltpu....  40.4 us

profile of v5, /device:TPU:8, one launch (start us, length us, event | category | flops | bytes accessed | tf_op | source)
XLA Modules:
  0.0 41.0 jit_solution(13420524419242873717)
XLA Ops:
  0.0 40.4 %decode_attention.1 = f32[16,80]{1,0:T(8,128)S(1)} custom-call(bf16[2,1024]{1,0:T(2,128)(2,1)} %q_hbm.1, s32[1,128]{1,0:T(1,128)} %bitcast.5, s32[2]{0:T(128)} %sl_hbm.1, bf16[512,128]{1,0:T(8,128)(2,1)} %k_hbm.1, bf16[512,128]{1,0:T(8,128)(2,1)} %v_hbm.1, f32[1,4]{1,0:T(1,128)} %bitcast.6, f32[1,4]{1,0:T(1,128)} %bitcast.7, bf16[2,256,128]{2,1,0:T(8,128)(2,1)} %sk_hbm.1, ...), custom_call_target="tpu_custom_call" | custom-call | tf_op jit(solution)/shard_map/decode_attention/pallas_call | solution.py:420
  40.4 0.6 %copy.12 = f32[16,80]{1,0:T(8,128)} copy(f32[16,80]{1,0:T(8,128)S(1)} %decode_attention.1) | data formatting | bytes 10240

commit v6 on v5

--- a/solution.py
+++ b/solution.py
@@ -210,7 +210,7 @@
     swap_v.wait_recv()
     swap_f.wait_recv()
 
-    chunk_chips = 8
+    chunk_chips = ROW_CHIPS
     chunk = chunk_chips * ROWS
     chunks = chips // chunk_chips
     row_in = lax.rem(lax.broadcasted_iota(jnp.int32, (chunk, WIDTH), 0), ROWS)
@@ -253,12 +253,11 @@
     own_chunk = chip // chunk_chips
 
     def chunk_step(k, carry):
-        off = lax.rem(k + chunks // 2, chunks)
-        n = lax.rem(own_chunk + off, chunks)
+        n = lax.rem(own_chunk + far_offset(k, chunks), chunks)
         prompt_chunk(n)
 
         def send_one(i, inner):
-            t = n * chunk_chips + (i // ROW_CHIPS) * ROW_CHIPS + far_in_row(lax.rem(i, ROW_CHIPS))
+            t = n * chunk_chips + far_in_row(i)
 
             @pl.when(t != chip)
             def _():
@@ -327,11 +326,8 @@
 
     for to in range(depth_chips):
         for b in range(ROW_CHIPS):
-            t = to * ROW_CHIPS + far_in_row(b)
-            if b < ROW_CHIPS - 1:
-                send_att(to, t)
-            else:
-                pl.when(t != chip)(functools.partial(send_att, to, t))
+            t = to * ROW_CHIPS + b
+            pl.when(t != chip)(functools.partial(send_att, to, t))
     load_w.wait()
     swap_w.wait_recv()
     per_group = ROW_CHIPS * OWN

time: 41.1 us -> 40.7 us (level)
  the two profiles are of different devices: /device:TPU:8 before, /device:TPU:1 now
where the time goes in v6:
time: 40.7 us; the launch traced here: 40.6 us
  Pallas kernels  40 us (98%)
  local copies, waits for them, and re-layouts  0.6 us (1%)
    pallas_call x1, Pallas kernels, local(): pl.pallas_call(functools.partial(kernel, chips, groups), out_shape=pltpu....  40 us

profile of v6, /device:TPU:1, one launch (start us, length us, event | category | flops | bytes accessed | tf_op | source)
XLA Modules:
  0.0 40.6 jit_solution(11667717083957699748)
XLA Ops:
  0.0 40.0 %decode_attention.1 = f32[16,80]{1,0:T(8,128)S(1)} custom-call(bf16[2,1024]{1,0:T(2,128)(2,1)} %q_hbm.1, s32[1,128]{1,0:T(1,128)} %bitcast.5, s32[2]{0:T(128)} %sl_hbm.1, bf16[512,128]{1,0:T(8,128)(2,1)} %k_hbm.1, bf16[512,128]{1,0:T(8,128)(2,1)} %v_hbm.1, f32[1,4]{1,0:T(1,128)} %bitcast.6, f32[1,4]{1,0:T(1,128)} %bitcast.7, bf16[2,256,128]{2,1,0:T(8,128)(2,1)} %sk_hbm.1, ...), custom_call_target="tpu_custom_call" | custom-call | tf_op jit(solution)/shard_map/decode_attention/pallas_call | solution.py:416
  40.0 0.6 %copy.12 = f32[16,80]{1,0:T(8,128)} copy(f32[16,80]{1,0:T(8,128)S(1)} %decode_attention.1) | data formatting | bytes 10240

commit v7 on v6

--- a/solution.py
+++ b/solution.py
@@ -296,7 +296,7 @@
 
     many_s = srecv.at[pl.ds(0, chips - 1)]
     remote(many_s, many_s, SS, partner, y).wait_recv()
-    stats = jnp.concatenate([srecv[i] for i in range(chips)], axis=0)
+    stats = srecv[...].reshape(chips, WIDTH)
     stats = jnp.concatenate([stats, jnp.zeros((WIDTH - chips, WIDTH), F32)], axis=0)
     stats = jnp.transpose(stats)
     peaks = stats[0:ROWS, 0:chips]
@@ -307,10 +307,12 @@
     total = jnp.sum(factor * totals, axis=1, keepdims=True) + near_total * near_factor
     many_n = nrecv.at[pl.ds(0, chips - 1)]
     remote(many_n, many_n, SN, partner, y).wait_recv()
-    numer = near_numer * near_factor
+    chains = [near_numer * near_factor] + [None] * 3
     for i in range(chips):
-        numer = numer + nrecv[i].astype(F32) * factor[:, i : i + 1]
-    att[chip] = (numer / total).astype(BF16)
+        term = nrecv[i].astype(F32) * factor[:, i : i + 1]
+        chains[i % 4] = term if chains[i % 4] is None else chains[i % 4] + term
+    numer = (chains[0] + chains[1]) + (chains[2] + chains[3])
+    att[chip] = (numer * (1.0 / total)).astype(BF16)
 
     row = chip // ROW_CHIPS
 

time: 40.7 us -> 40.7 us (level)
  no operation moved by 1% of the time
where the time goes in v7:
time: 40.7 us; the launch traced here: 40.6 us
  Pallas kernels  40 us (98%)
  local copies, waits for them, and re-layouts  0.6 us (1%)
    pallas_call x1, Pallas kernels, local(): pl.pallas_call(functools.partial(kernel, chips, groups), out_shape=pltpu....  40 us

profile of v7, /device:TPU:1, one launch (start us, length us, event | category | flops | bytes accessed | tf_op | source)
XLA Modules:
  0.0 40.6 jit_solution(14449013364958921103)
XLA Ops:
  0.0 40.0 %decode_attention.1 = f32[16,80]{1,0:T(8,128)S(1)} custom-call(bf16[2,1024]{1,0:T(2,128)(2,1)} %q_hbm.1, s32[1,128]{1,0:T(1,128)} %bitcast.5, s32[2]{0:T(128)} %sl_hbm.1, bf16[512,128]{1,0:T(8,128)(2,1)} %k_hbm.1, bf16[512,128]{1,0:T(8,128)(2,1)} %v_hbm.1, f32[1,4]{1,0:T(1,128)} %bitcast.6, f32[1,4]{1,0:T(1,128)} %bitcast.7, bf16[2,256,128]{2,1,0:T(8,128)(2,1)} %sk_hbm.1, ...), custom_call_target="tpu_custom_call" | custom-call | tf_op jit(solution)/shard_map/decode_attention/pallas_call | solution.py:418
  40.0 0.6 %copy.12 = f32[16,80]{1,0:T(8,128)} copy(f32[16,80]{1,0:T(8,128)S(1)} %decode_attention.1) | data formatting | bytes 10240
